TPU v7x, 256 devices: a whole 4x4x8 slice. The times are simulated.
256 devices in a mesh: blk: 16 (over z_hi, y, core), rep: 16 (over z_lo, x).
Axes of the slice: x: 4, y: 4, z: 8 (z_hi: 2, z_lo: 4; z = z_hi * 4 + z_lo), core: 2. Of those that a mesh axis runs over, the one named last changes fastest.
Arguments:
- query_rows: bfloat16 [114688, 2560], P(('blk', 'rep')), may hold values from -6 to 6
- key_rows: bfloat16 [114688, 2560], P(('blk', 'rep')), may hold values from -6 to 6
- value_rows: bfloat16 [114688, 2560], P(('blk', 'rep')), may hold values from -24 to 24
- cotangent: bfloat16 [114688, 2560], P(('blk', 'rep')), may hold values from -0.0625 to 0.0625
- out_weight: bfloat16 [2560, 2560], P('blk'), may hold values from -0.125 to 0.125
- first_moment: float32 [2560, 2560], P(('blk', 'rep')), may hold values from -6 to 6
- second_moment: float32 [2560, 2560], P(('blk', 'rep')), may hold values from 0.5 to 4
Outputs:
- projected: bfloat16 [114688, 2560], P(('blk', 'rep'))
- first_next: float32 [2560, 2560], P(('blk', 'rep'))
- second_next: float32 [2560, 2560], P(('blk', 'rep'))
All inputs are finite; a program needn't handle non-finite values.
Results may differ from a plain program's by a relative error of at most 0.015.
Values may be sent and summed in bfloat16 or wider, within the bound.
A program may use at most 192 MiB of HBM per device.

v0:
```python
import math

import jax
import jax.numpy as jnp
from jax import lax
from jax.sharding import PartitionSpec as P

HEADS = 20
HD = 128


NEG = -1e30


def attend(query_part, key_part, value_part):
    length = query_part.shape[0]
    q = query_part.reshape(length, HEADS, HD)
    k = key_part.reshape(length, HEADS, HD)
    v = value_part.reshape(length, HEADS, HD)
    scores = jnp.einsum("qhd,khd->hqk", q, k, preferred_element_type=jnp.float32) * (
        1.0 / math.sqrt(HD)
    )
    later = lax.broadcasted_iota(jnp.int32, (length, length), 1) > lax.broadcasted_iota(
        jnp.int32, (length, length), 0
    )
    scores = jnp.where(later[None, :, :], NEG, scores)
    top = jnp.max(scores, axis=-1, keepdims=True)
    expo = jnp.exp(scores - top)
    probs = (expo / jnp.sum(expo, axis=-1, keepdims=True)).astype(jnp.bfloat16)
    context = jnp.einsum("hqk,khd->qhd", probs, v, preferred_element_type=jnp.float32)
    return context.reshape(length, HEADS * HD).astype(jnp.bfloat16)


def on_device(query_rows, key_rows, value_rows, cotangent, out_weight, first_moment, second_moment):
    context = attend(query_rows, key_rows, value_rows)
    columns = context
    summed = jnp.dot(
        columns,
        lax.all_gather(out_weight, "blk", axis=0, tiled=True),
        preferred_element_type=jnp.float32,
    )
    projected = summed.astype(jnp.bfloat16)
    share_rows = first_moment.shape[0]
    columns = context
    term = lax.dot_general(
        columns, cotangent, (((0,), (0,)), ((), ())), preferred_element_type=jnp.float32
    )
    block_grad = lax.psum_scatter(
        lax.optimization_barrier(term.astype(jnp.bfloat16))
        .astype(jnp.float32)
        .astype(jnp.bfloat16),
        "blk",
        scatter_dimension=0,
        tiled=True,
    ).astype(jnp.float32)
    whole_grad = lax.psum(block_grad, "rep")
    gradient = lax.dynamic_slice_in_dim(
        whole_grad, lax.axis_index("rep") * share_rows, share_rows, 0
    )
    first_next = 0.9 * first_moment + 0.1 * gradient
    second_next = 0.95 * second_moment + 0.05 * gradient * gradient
    return (projected, first_next, second_next)


def solution(mesh):
    in_specs = (
        P(("blk", "rep"), None),
        P(("blk", "rep"), None),
        P(("blk", "rep"), None),
        P(("blk", "rep"), None),
        P("blk", None),
        P(("blk", "rep"), None),
        P(("blk", "rep"), None),
    )
    out_specs = (P(("blk", "rep"), None), P(("blk", "rep"), None), P(("blk", "rep"), None))
    return jax.shard_map(
        on_device, mesh=mesh, in_specs=in_specs, out_specs=out_specs, check_vma=False
    )
```

profile of v0, /device:TPU:65, one launch (start us, length us, event | category | flops | bytes accessed | tf_op | source)
XLA Modules:
  0.0 402.6 jit_solution(9935982141337449768)
XLA Ops:
  7.2 0.0 copy-start
  7.2 0.0 reduce-scatter.2.cloned.1.call-start
  7.2 0.1 iota_compare_fusion
  7.3 12.2 %fusion.38 = (f32[20,448]{1,0:T(8,128)S(1)}, f32[20,448,448]{1,2,0:T(8,128)}) fusion(pred[448,448]{0,1:T(8,128)(4,1)S(1)} %iota_compare_fusion, bf16[448,2560]{1,0:T(8,128)(2,1)} %param.8, bf16[448,2560]{1,0:T(8,128)(2,1)} %param.7), kind=kOutput, calls=%fused_computation.34 | convolution fusion | flops 1043661248 | bytes 20880384 | tf_op jit(solution)/shard_map/sub | solution.py:28
  19.5 8.5 %convert_bitcast_fusion = bf16[20,56,8,128]{3,2,1,0:T(8,128)(2,1)S(1)} fusion(f32[20,448,448]{1,2,0:T(8,128)} %get-tuple-element.6, f32[20,448]{1,0:T(8,128)S(1)} %get-tuple-element.5, bf16[448,2560]{1,0:T(8,128)(2,1)} %param.9), kind=kOutput, calls=%fused_computation.21 | convolution fusion | flops 1036779520 | bytes 20679680 | tf_op jit(solution)/shard_map/hqk,khd->qhd/dot_general | solution.py:30
  28.0 0.0 copy-start.3
  28.0 1.4 copy-done.3
  29.4 0.0 copy-done
  29.4 10.0 %convolution_convert_fusion = bf16[2560,2560]{1,0:T(8,128)(2,1)} fusion(bf16[448,2560]{1,0:T(8,128)(2,1)S(1)} %copy-done, bf16[20,56,8,128]{3,2,1,0:T(8,128)(2,1)S(1)} %convert_bitcast_fusion), kind=kOutput, calls=%fused_computation.4 | convolution fusion | flops 5878579200 | bytes 17694720 | tf_op jit(solution)/shard_map/dot_general | solution.py:45
  39.4 0.0 reduce-scatter.2.cloned.1.call-update
  39.4 0.0 copy-start.1
  39.4 0.0 copy-start.2
  39.4 0.0 all-gather.2.cloned.1.call-start
  39.5 0.7 all-gather.2.cloned.1.call-update
  40.2 180.6 %reduce-scatter.2.cloned.1.call-done = bf16[160,2560]{1,0:T(8,128)(2,1)} async-done(((bf16[2560,2560]{1,0:T(8,128)(2,1)}), bf16[160,2560]{1,0:T(8,128)(2,1)}) %reduce-scatter.2.cloned.1.call-update) | async-done | bytes 819216 | tf_op jit(solution)/shard_map/reduce_scatter | solution.py:48
  220.8 95.4 %all-reduce.1 = f32[160,2560]{1,0:T(8,128)} all-reduce(bf16[160,2560]{1,0:T(8,128)(2,1)} %reduce-scatter.2.cloned.1.call-done), channel_id=1, replica_groups=mesh['blk'=16,'rep'=16] {'rep'}, use_global_device_ids=true, to_apply=%region_3.4 | all-reduce | flops 409600 | bytes 2457600 | tf_op jit(solution)/shard_map/psum | solution.py:56
  316.2 0.0 copy-done.1
  316.2 0.0 copy-done.2
  316.2 1.7 fusion.35
  317.9 67.0 %all-gather.2.cloned.1.call-done = bf16[2560,2560]{1,0:T(8,128)(2,1)} async-done(((bf16[160,2560]{1,0:T(8,128)(2,1)}), bf16[2560,2560]{1,0:T(8,128)(2,1)}) %all-gather.2.cloned.1.call-update) | async-done | bytes 13107216 | tf_op jit(solution)/shard_map/all_gather | solution.py:39
  384.9 10.8 %convolution_convert_fusion.1 = bf16[448,2560]{1,0:T(8,128)(2,1)} fusion(bf16[2560,2560]{1,0:T(8,128)(2,1)} %all-gather.2.cloned.1.call-done, bf16[20,56,8,128]{3,2,1,0:T(8,128)(2,1)} %copy-done.3), kind=kOutput, calls=%fused_computation.11 | convolution fusion | flops 5873172480 | bytes 17694720 | tf_op jit(solution)/shard_map/dot_general | solution.py:37
Async XLA Ops:
  7.2 22.2 %copy-start = (bf16[448,2560]{1,0:T(8,128)(2,1)S(1)}, bf16[448,2560]{1,0:T(8,128)(2,1)}, u32[]{:S(2)}) copy-start(bf16[448,2560]{1,0:T(8,128)(2,1)} %param.10) | copy-start | bytes 6881284
  7.2 213.6 %reduce-scatter.2.cloned.1.call-start = ((), (), s32[]{:S(2)}) async-start(), calls=%async_computation.2 | async-start | bytes 13926400 | tf_op jit(solution)/shard_map/reduce_scatter | solution.py:48
  28.0 1.4 copy-start.3
  39.4 276.8 %copy-start.1 = (f32[10,2560]{1,0:T(8,128)S(1)}, f32[10,2560]{1,0:T(8,128)}, u32[]{:S(2)}) copy-start(f32[10,2560]{1,0:T(8,128)} %param.13) | copy-start | bytes 307204
  39.4 276.7 %copy-start.2 = (f32[10,2560]{1,0:T(8,128)S(1)}, f32[10,2560]{1,0:T(8,128)}, u32[]{:S(2)}) copy-start(f32[10,2560]{1,0:T(8,128)} %param.12) | copy-start | bytes 307204
  39.4 345.5 %all-gather.2.cloned.1.call-start = ((), (), s32[]{:S(2)}) async-start(), calls=%async_computation.1 | async-start | bytes 13926400 | tf_op jit(solution)/shard_map/all_gather | solution.py:39
Sparse Core Ops, SparseCore 0:
  39.5 181.2 reduce-scatter.1
  223.5 161.3 all-gather.1
where the time goes:
time: 403 us
  waiting for transfers between devices  248 us (62%)
  blocking collectives  95.4 us (24%)
  matrix products  41.5 us (10%)
  between operations  14.1 us (3%)
    reduce_scatter x1, waiting for transfers between devices, on_device(): lax.psum_scatter(lax.optimization_barrier(term.astype(jnp.bfloat16)).asty...  181 us
    psum x1, blocking collectives, on_device(): whole_grad = lax.psum(block_grad, 'rep')  95.4 us
    all_gather x1, waiting for transfers between devices, on_device(): lax.all_gather(out_weight, 'blk', axis=0, tiled=True)  67 us
    sub x1, matrix products, attend(): expo = jnp.exp(scores - top)  12.2 us
    dot_general x1, matrix products, on_device(): jnp.dot(columns, lax.all_gather(out_weight, 'blk', axis=0, tiled=True), p...  10.8 us
    dot_general x1, matrix products, on_device(): lax.dot_general(columns, cotangent, (((0,), (0,)), ((), ())), preferred_e...  10 us
    dot_general x1, matrix products, attend(): jnp.einsum('hqk,khd->qhd', probs, v, preferred_element_type=jnp.float32)  8.52 us
  transfers between devices with their start and end apart: 2, of which 2 were waited for; matrix products, arithmetic and copies ran while one was open for 0% of the time, Pallas kernels for 0%

commit v1 on v0

v1 whole, which is shorter than its diff:
```python
import functools
import math

import jax
import jax.numpy as jnp
from jax import lax
from jax.experimental import pallas as pl
from jax.experimental.pallas import tpu as pltpu
from jax.sharding import PartitionSpec as P

HEADS = 20
HD = 128
SEQ = 448
D = 2560
NEG = -1e30
BF = jnp.bfloat16
F32 = jnp.float32
MESH = pl.DeviceIdType.MESH
WA, WB, WC = 48, 32, 80
Q4 = D // 4
NSEM = 110
SCALE = math.log2(math.e) / math.sqrt(HD)
QBLOCKS = ((0, 128), (128, 128), (256, 128), (384, 64))


def ring(value, shift, size):
    return lax.rem(value + shift + size, size)


def kernel(q_hbm, k_hbm, v_hbm, t_hbm, w_hbm, m1_hbm, m2_hbm,
           out_hbm, first_hbm, second_hbm,
           qs, ks, vs, ct, cto, ctx, ctt, cxo, wf, go, r1x, r2x, r1y, r2y, r3a, r3b, pc, rz, s3, snd, r4,
           m1, m2, ss, rs, ls):
    blk = lax.axis_index("blk")
    rep = lax.axis_index("rep")
    zh, y, c = blk // 8, lax.rem(blk // 2, 4), lax.rem(blk, 2)
    zl, x = rep // 4, lax.rem(rep, 4)
    z = zh * 4 + zl
    oz, oc = 1 - zh, 1 - c

    def at(xx, yy, zz, cc):
        return (zz // 4) * 8 + yy * 2 + cc, lax.rem(zz, 4) * 4 + xx

    def dx(s):
        return at(ring(x, s, 4), y, z, c)

    def dy(s):
        return at(x, ring(y, s, 4), z, c)

    def dz(s):
        return at(x, y, ring(z, s, 8), c)

    sib = at(x, y, z, oc)

    count = [0]
    sent = []

    def send(src, dst, dev):
        i = count[0]
        count[0] += 1
        cp = pltpu.make_async_remote_copy(
            src_ref=src, dst_ref=dst, send_sem=ss.at[i], recv_sem=rs.at[i],
            device_id=dev, device_id_type=MESH)
        cp.start()
        sent.append(cp)
        return cp

    def local(i, src, dst):
        cp = pltpu.make_async_copy(src, dst, ls.at[i])
        cp.start()
        return cp

    lw = local(0, w_hbm, wf.at[zh, y, c])
    lt = local(1, t_hbm, ct)
    lq = local(2, q_hbm, qs)
    lk = local(3, k_hbm, ks)
    lv = local(4, v_hbm, vs)
    lm1 = local(5, m1_hbm, m1)
    lm2 = local(6, m2_hbm, m2)

    lw.wait()
    barrier = pltpu.get_barrier_semaphore()
    partners = [dx(1), dx(2), dx(3), dy(1), dy(2), dy(3)] + [dz(s) for s in range(1, 8)] + [sib]
    for dev in partners:
        pl.semaphore_signal(barrier, inc=1, device_id=dev, device_id_type=MESH)
    pl.semaphore_wait(barrier, len(partners))

    def cols(quarter):
        return pl.ds(pl.multiple_of(quarter * Q4, 128), Q4)

    ra, rb, rc = pl.ds(0, WA), pl.ds(WA, WB), pl.ds(WA + WB, WC)

    def give(dev, *region):
        ref = wf.at[region]
        return send(ref, ref, dev)

    c1 = [give(dy(s), zh, y, c, rc, cols(zl)) for s in (1, 3, 2)]
    a1 = give(dz(4), zh, y, c, pl.ds(0, WA + WB), cols(x))
    a2o = [give(dy(s), zh, y, c, ra, cols(x)) for s in (1, 3, 2)]
    b3o = [give(dy(1), zh, y, c, rb, pl.ds(0, D)), give(dy(3), zh, y, c, rb, pl.ds(0, D))]
    lt.wait()
    tsend = send(ct, cto, sib)
    lq.wait()
    lk.wait()
    lv.wait()

    def attend(h, carry):
        off = pl.multiple_of(h * HD, HD)
        lane = pl.ds(off, HD)
        for q0, qn in QBLOCKS:
            kn = q0 + qn
            s = lax.dot_general(qs[pl.ds(q0, qn), lane], ks[pl.ds(0, kn), lane],
                                (((1,), (1,)), ((), ())), preferred_element_type=F32)
            later = lax.broadcasted_iota(jnp.int32, (qn, kn), 1) > lax.broadcasted_iota(
                jnp.int32, (qn, kn), 0) + q0
            s = jnp.where(later, NEG, s)
            top = jnp.max(s, axis=-1, keepdims=True)
            p = jnp.exp2((s - top) * SCALE)
            total = jnp.sum(p, axis=-1, keepdims=True)
            o = lax.dot_general(p.astype(BF), vs[pl.ds(0, kn), lane],
                                (((1,), (0,)), ((), ())), preferred_element_type=F32)
            o = o * (1.0 / total)
            ctx[pl.ds(q0, qn), lane] = o.astype(BF)
            ctt[pl.ds(off, HD), pl.ds(q0, qn)] = o.T.astype(BF)
        return carry

    def heads(lo, hi):
        lax.fori_loop(lo, hi, attend, 0)

    def rows_of(zz, yy, cc):
        return pl.ds(pl.multiple_of((zz * 8 + yy * 2 + cc) * 160, 32), 160)

    heads(0, 5)
    for cp in c1:
        cp.wait_recv()
    every = pl.ds(0, 4)
    c2 = [[give(dz(1), zh, every, c, rc, cols(zl)), give(dz(7), zh, every, c, rc, cols(zl))]]
    sibs = [give(sib, zh, every, c, rc, cols(zl))]
    a1.wait_recv()
    b2 = [give(dx(s), oz, y, c, rb, cols(x)) for s in (1, 3, 2)]
    a2t = [give(dy(s), oz, y, c, ra, cols(x)) for s in (1, 3, 2)]
    heads(5, 10)
    for cp in a2o:
        cp.wait_recv()
    a3o = [give(dx(1), zh, every, c, ra, cols(x)), give(dx(3), zh, every, c, ra, cols(x))]
    for cp in b2:
        cp.wait_recv()
    b3t = [give(dy(1), oz, y, c, rb, pl.ds(0, D)), give(dy(3), oz, y, c, rb, pl.ds(0, D))]
    heads(10, 15)
    half = (pl.ds(0, D // 2), pl.ds(D // 2, D // 2))
    b3o[0].wait_recv()
    fo = [give(dy(1), zh, ring(y, -1, 4), c, rb, half[0])]
    b3o[1].wait_recv()
    fo.append(give(dy(3), zh, ring(y, 1, 4), c, rb, half[1]))

    def zpos(s):
        zz = ring(z, s, 8)
        return zz // 4, lax.rem(zz, 4)

    def zstep(step):
        prev = c2[step - 1]
        nxt = []
        for side, cp in enumerate(prev):
            cp.wait_recv()
            hh, ll = zpos(-step if side == 0 else step)
            if step < 3:
                part = every
            else:
                part = pl.ds(0, 2) if side == 0 else pl.ds(2, 2)
            nxt.append(give(dz(1 if side == 0 else 7), hh, part, c, rc, cols(ll)))
            sibs.append(give(sib, hh, every, c, rc, cols(ll)))
        c2.append(nxt)

    zstep(1)
    heads(15, 20)
    xs = [send(ctt.at[rows_of(zz, yy, oc)], cxo.at[zz, yy], sib) for zz in range(2) for yy in range(4)]
    for cp in a2t:
        cp.wait_recv()
    a3t = [give(dx(1), oz, every, c, ra, cols(x)), give(dx(3), oz, every, c, ra, cols(x))]
    for cp in b3t:
        cp.wait_recv()
    ft = [give(dy(1), oz, ring(y, -1, 4), c, rb, half[0]), give(dy(3), oz, ring(y, 1, 4), c, rb, half[1])]

    tsend.wait_recv()

    xp, xo, xm = ring(x, 1, 4), ring(x, 2, 4), ring(x, 3, 4)
    yp, yo, ym = ring(y, 1, 4), ring(y, 2, 4), ring(y, 3, 4)
    ga, gb = pl.ds(0, 80), pl.ds(80, 80)
    alld = pl.ds(0, D)

    def grads(zz):
        for cp in xs[zz * 4:zz * 4 + 4]:
            cp.wait_recv()

        def tile(n, carry):
            lane = pl.ds(pl.multiple_of(n * 512, 128), 512)
            mine = jnp.concatenate([ctt[rows_of(zz, yy, c), :] for yy in range(4)], axis=0)
            acc = jnp.dot(mine, ct[:, lane], preferred_element_type=F32)
            acc += jnp.dot(cxo[zz].reshape(640, SEQ), cto[:, lane], preferred_element_type=F32)
            go[zz, :, :, lane] = acc.astype(BF).reshape(4, 160, 512)
            return carry

        lax.fori_loop(0, 5, tile, 0)

    grads(0)
    s1xp = send(go.at[0, every, ga, cols(xo)], r1x.at[0], dx(1))
    s1yp = send(go.at[0, yo, gb, alld], r1y.at[0], dy(1))
    oxm = send(go.at[0, every, ga, cols(xm)], r2x.at[1, 0], dx(3))
    oym = send(go.at[0, ym, gb, alld], r2y.at[1, 0], dy(3))
    a3o[0].wait_recv()
    fa = []
    ah = (pl.ds(0, 2), pl.ds(2, 2))
    fa.append(give(dx(1), zh, ah[0], c, ra, cols(xm)))
    a3o[1].wait_recv()
    fa.append(give(dx(3), zh, ah[1], c, ra, cols(xp)))
    grads(1)
    s1xm = send(go.at[1, every, ga, cols(xo)], r1x.at[1], dx(3))
    s1ym = send(go.at[1, yo, gb, alld], r1y.at[1], dy(3))
    oxp = send(go.at[1, every, ga, cols(xp)], r2x.at[0, 1], dx(1))
    oyp = send(go.at[1, yp, gb, alld], r2y.at[0, 1], dy(1))

    zstep(2)
    for cp in fo:
        cp.wait_recv()
    sibs.append(give(sib, zh, every, c, rb, alld))
    for cp in ft:
        cp.wait_recv()
    sibs.append(give(sib, oz, every, c, rb, alld))
    a3t[0].wait_recv()
    fa.append(give(dx(1), oz, ah[0], c, ra, cols(xm)))
    a3t[1].wait_recv()
    fa.append(give(dx(3), oz, ah[1], c, ra, cols(xp)))

    def addf(*parts):
        total = parts[0].astype(F32)
        for part in parts[1:]:
            total = total + part.astype(F32)
        return total.astype(BF)

    s1xp.wait_recv()
    for yy in range(4):
        go[0, yy, ga, cols(xp)] = addf(go[0, yy, ga, cols(xp)], r1x[0, yy])
    s2xp = send(go.at[0, every, ga, cols(xp)], r2x.at[0, 0], dx(1))
    s1yp.wait_recv()
    go[0, yp, gb, :] = addf(go[0, yp, gb, :], r1y[0])
    s2yp = send(go.at[0, yp, gb, alld], r2y.at[0, 0], dy(1))
    s1xm.wait_recv()
    for yy in range(4):
        go[1, yy, ga, cols(xm)] = addf(go[1, yy, ga, cols(xm)], r1x[1, yy])
    s2xm = send(go.at[1, every, ga, cols(xm)], r2x.at[1, 1], dx(3))
    s1ym.wait_recv()
    go[1, ym, gb, :] = addf(go[1, ym, gb, :], r1y[1])
    s2ym = send(go.at[1, ym, gb, alld], r2y.at[1, 1], dy(3))

    for cp in fa:
        cp.wait_recv()
    sibs.append(give(sib, zh, every, c, ra, alld))
    sibs.append(give(sib, oz, every, c, ra, alld))
    zstep(3)
    for cp in c2[3]:
        cp.wait_recv()
    hh, ll = zpos(4)
    sibs.append(give(sib, hh, every, c, rc, cols(ll)))
    for cp in sibs:
        cp.wait_recv()

    outs = []
    for n in range(10):
        lane = pl.ds(n * 256, 256)
        w = wf[:, :, :, :, lane].reshape(D, 256)
        qs[:, lane] = jnp.dot(ctx[...], w, preferred_element_type=F32).astype(BF)
    outs.append(local(7, qs, out_hbm))

    for cp in (oxm, oxp, s2xp, s2xm):
        cp.wait_recv()
    for zz in range(2):
        for yy in range(4):
            go[zz, yy, ga, cols(x)] = addf(go[zz, yy, ga, cols(x)], r2x[0, zz, yy], r2x[1, zz, yy])
    both = pl.ds(0, 2)
    p2a = [send(go.at[both, ring(y, s, 4), ga, cols(x)], r3a.at[s - 1], dy(s)) for s in (1, 3, 2)]
    for cp in (oym, oyp, s2yp, s2ym):
        cp.wait_recv()
    for zz in range(2):
        go[zz, y, gb, :] = addf(go[zz, y, gb, :], r2y[0, zz], r2y[1, zz])
    p2b = [send(go.at[both, y, gb, cols(ring(x, s, 4))], r3b.at[s - 1], dx(s)) for s in (1, 3, 2)]
    for cp in p2a:
        cp.wait_recv()
    for zz in range(2):
        pc[zz, ga, :] = addf(go[zz, y, ga, cols(x)], r3a[0, zz], r3a[1, zz], r3a[2, zz])
    for cp in p2b:
        cp.wait_recv()
    for zz in range(2):
        pc[zz, gb, :] = addf(go[zz, y, gb, cols(x)], r3b[0, zz], r3b[1, zz], r3b[2, zz])

    def window(ll):
        return pl.ds(pl.multiple_of(ll * 40 - 8 * lax.rem(ll, 2), 16), 48)

    p3 = []
    for s in (4, 3, 5, 2, 6, 1, 7):
        hh, ll = zpos(s)
        p3.append(send(pc.at[hh, window(ll), :], rz.at[s - 1], dz(s)))
    for cp in p3:
        cp.wait_recv()
    total = pc[zh, window(zl), :].astype(F32)
    for s in range(7):
        total = total + rz[s].astype(F32)
    s3[...] = total

    mine = s3[pl.ds(pl.multiple_of(8 * lax.rem(zl, 2), 8), 40), :]
    snd[...] = jnp.zeros(snd.shape, F32)
    for t in range(4):
        snd[t, pl.ds(0, 10), :] = mine[10 * t:10 * t + 10, :]
    p4 = [send(snd.at[ring(x, s, 4)], r4.at[s - 1], dx(s)) for s in (1, 3, 2)]
    lm1.wait()
    lm2.wait()

    def adam(quarter, g):
        lane = cols(quarter)
        m1[:, lane] = 0.9 * m1[:, lane] + 0.1 * g
        m2[:, lane] = 0.95 * m2[:, lane] + 0.05 * g * g

    adam(x, snd[x, pl.ds(0, 10), :])
    for s, cp in zip((1, 3, 2), p4):
        cp.wait_recv()
        adam(ring(x, -s, 4), r4[s - 1, pl.ds(0, 10), :])
    outs.append(local(8, m1, first_hbm))
    outs.append(local(9, m2, second_hbm))
    for cp in sent:
        cp.wait_send()
    for cp in outs:
        cp.wait()
    assert count[0] <= NSEM, count[0]


def on_device(*args):
    any_spec = pl.BlockSpec(memory_space=pl.ANY)
    V = pltpu.VMEM
    return pl.pallas_call(
        kernel,
        name="fused_layer",
        out_shape=(
            jax.ShapeDtypeStruct((SEQ, D), BF),
            jax.ShapeDtypeStruct((10, D), F32),
            jax.ShapeDtypeStruct((10, D), F32),
        ),
        in_specs=[any_spec] * 7,
        out_specs=(any_spec,) * 3,
        scratch_shapes=[
            V((SEQ, D), BF), V((SEQ, D), BF), V((SEQ, D), BF), V((SEQ, D), BF), V((SEQ, D), BF),
            V((SEQ, D), BF),
            V((D, SEQ), BF),
            V((2, 4, 160, SEQ), BF),
            V((2, 4, 2, 160, D), BF),
            V((2, 4, 160, D), BF),
            V((2, 4, 80, Q4), BF),
            V((2, 2, 4, 80, Q4), BF),
            V((2, 80, D), BF),
            V((2, 2, 80, D), BF),
            V((3, 2, 80, Q4), BF),
            V((3, 2, 80, Q4), BF),
            V((2, 160, Q4), BF),
            V((7, 48, Q4), BF),
            V((48, Q4), F32),
            V((4, 16, Q4), F32),
            V((3, 16, Q4), F32),
            V((10, D), F32), V((10, D), F32),
            pltpu.SemaphoreType.DMA((NSEM,)),
            pltpu.SemaphoreType.DMA((NSEM,)),
            pltpu.SemaphoreType.DMA((10,)),
        ],
        compiler_params=pltpu.CompilerParams(
            collective_id=0, has_side_effects=True, vmem_limit_bytes=60 * 2**20),
        cost_estimate=pl.CostEstimate(flops=15_000_000_000, bytes_accessed=14_000_000, transcendentals=2_600_000),
    )(*args)


def solution(mesh):
    rows = P(("blk", "rep"), None)
    return jax.shard_map(
        on_device, mesh=mesh, in_specs=(rows, rows, rows, rows, P("blk", None), rows, rows),
        out_specs=(rows, rows, rows), check_vma=False)
```

time: 403 us -> 119 us (0.30)
  the two profiles are of different devices: /device:TPU:65 before, /device:TPU:1 now
where the time goes in v1:
time: 119 us
  Pallas kernels  114 us (96%)
  local copies, waits for them, and re-layouts  4.56 us (4%)
    pallas_call x1, Pallas kernels, on_device(): pl.pallas_call(kernel, name='fused_layer', out_shape=(jax.ShapeDtypeStruc...  114 us
    unnamed x7, local copies, waits for them, and re-layouts  4.56 us

profile of v1, /device:TPU:1, one launch (start us, length us, event | category | flops | bytes accessed | tf_op | source)
XLA Modules:
  0.0 118.9 jit_solution(11104186160518610396)
XLA Ops:
  0.6 113.7 %fused_layer.1 = (bf16[448,2560]{1,0:T(8,128)(2,1)}, f32[10,2560]{1,0:T(8,128)}, f32[10,2560]{1,0:T(8,128)}) custom-call(bf16[448,2560]{1,0:T(8,128)(2,1)} %q_hbm.1, bf16[448,2560]{1,0:T(8,128)(2,1)} %k_hbm.1, bf16[448,2560]{1,0:T(8,128)(2,1)} %v_hbm.1, bf16[448,2560]{1,0:T(8,128)(2,1)} %t_hbm.1, bf16[160,2560]{1,0:T(8,128)(2,1)} %w_hbm.1, ...), custom_call_target="tpu_custom_call" | custom-call | flops 15000000512 | bytes 14000000 | tf_op jit(solution)/shard_map/fused_layer/pallas_call | solution.py:338
  114.3 0.0 copy-start.1
  114.3 0.0 copy-start
  114.3 3.2 %copy.13 = bf16[448,2560]{1,0:T(8,128)(2,1)} copy(bf16[448,2560]{1,0:T(8,128)(2,1)} %get-tuple-element.6) | data formatting | bytes 4587520
  117.6 0.0 copy-done.1
  117.6 0.7 copy.14
  118.2 0.0 copy-done
  118.2 0.7 copy.15
Async XLA Ops:
  114.3 3.2 %copy-start.1 = (f32[10,2560]{1,0:T(8,128)S(1)}, f32[10,2560]{1,0:T(8,128)}, u32[]{:S(2)}) copy-start(f32[10,2560]{1,0:T(8,128)} %get-tuple-element.7) | copy-start | bytes 307204
  114.3 3.9 %copy-start = (f32[10,2560]{1,0:T(8,128)S(1)}, f32[10,2560]{1,0:T(8,128)}, u32[]{:S(2)}) copy-start(f32[10,2560]{1,0:T(8,128)} %get-tuple-element.8) | copy-start | bytes 307204

commit v2 on v1

v2 whole, which is shorter than its diff:
```python
import functools
import math

import jax
import jax.numpy as jnp
from jax import lax
from jax.experimental import pallas as pl
from jax.experimental.pallas import tpu as pltpu
from jax.sharding import PartitionSpec as P

HEADS = 20
HD = 128
SEQ = 448
D = 2560
NEG = -1e30
BF = jnp.bfloat16
F32 = jnp.float32
MESH = pl.DeviceIdType.MESH
WA, WB, WC = 32, 16, (64, 48)
Q4 = D // 4
NSEM = 160
CHUNKS = ((0, 48), (48, 32))
SCALE = math.log2(math.e) / math.sqrt(HD)
QBLOCKS = ((0, 256), (256, 192))


def ring(value, shift, size):
    return lax.rem(value + shift + size, size)


def kernel(q_hbm, k_hbm, v_hbm, t_hbm, w_hbm, m1_hbm, m2_hbm,
           out_ref, first_ref, second_ref,
           qs, ks, vs, ct, cto, ctx, ctt, cxo, wf, go, r1x, r2x, r1y, r2y, r3a, r3b, pc, rz, s3, snd, r4,
           m1, m2, ss, rs, ls):
    blk = lax.axis_index("blk")
    rep = lax.axis_index("rep")
    zh, y, c = blk // 8, lax.rem(blk // 2, 4), lax.rem(blk, 2)
    zl, x = rep // 4, lax.rem(rep, 4)
    z = zh * 4 + zl
    oz, oc = 1 - zh, 1 - c

    def at(xx, yy, zz, cc):
        return (zz // 4) * 8 + yy * 2 + cc, lax.rem(zz, 4) * 4 + xx

    def dx(s):
        return at(ring(x, s, 4), y, z, c)

    def dy(s):
        return at(x, ring(y, s, 4), z, c)

    def dz(s):
        return at(x, y, ring(z, s, 8), c)

    sib = at(x, y, z, oc)

    count = [0]
    sent = []

    def send(src, dst, dev):
        i = count[0]
        count[0] += 1
        cp = pltpu.make_async_remote_copy(
            src_ref=src, dst_ref=dst, send_sem=ss.at[i], recv_sem=rs.at[i],
            device_id=dev, device_id_type=MESH)
        cp.start()
        sent.append(cp)
        return cp

    def local(i, src, dst):
        cp = pltpu.make_async_copy(src, dst, ls.at[i])
        cp.start()
        return cp

    lw = local(0, w_hbm, wf.at[zh, y, c])
    lt = local(1, t_hbm, ct)
    lq = local(2, q_hbm, qs)
    lk = local(3, k_hbm, ks)
    lv = local(4, v_hbm, vs)
    lm1 = local(5, m1_hbm, m1)
    lm2 = local(6, m2_hbm, m2)

    lw.wait()
    barrier = pltpu.get_barrier_semaphore()
    partners = [dx(1), dx(2), dx(3), dy(1), dy(2), dy(3)] + [dz(s) for s in range(1, 8)] + [sib]
    for dev in partners:
        pl.semaphore_signal(barrier, inc=1, device_id=dev, device_id_type=MESH)
    pl.semaphore_wait(barrier, len(partners))

    def cols(quarter):
        return pl.ds(pl.multiple_of(quarter * Q4, 128), Q4)

    ra, rb = pl.ds(0, WA), pl.ds(WA, WB)
    rc = (pl.ds(WA + WB, WC[0]), pl.ds(WA + WB + WC[0], WC[1]))

    def give(dev, *region):
        ref = wf.at[region]
        return send(ref, ref, dev)

    a2o = [give(dy(s), zh, y, c, ra, cols(x)) for s in (1, 3, 2)]
    a1 = give(dz(4), zh, y, c, pl.ds(0, WA + WB), cols(x))
    c1 = [[give(dy(s), zh, y, c, rc[0], cols(zl)) for s in (1, 3, 2)]]
    b3o = [give(dy(1), zh, y, c, rb, pl.ds(0, D)), give(dy(3), zh, y, c, rb, pl.ds(0, D))]
    c1.append([give(dy(s), zh, y, c, rc[1], cols(zl)) for s in (1, 3, 2)])
    lt.wait()
    tsend = send(ct, cto, sib)
    lq.wait()
    lk.wait()
    lv.wait()

    def attend(i, carry):
        work = []
        for j in range(4):
            off = pl.multiple_of((i * 4 + j) * HD, HD)
            for q0, qn in QBLOCKS:
                work.append((off, pl.ds(off, HD), q0, qn, q0 + qn))
        scores = []
        for off, lane, q0, qn, kn in work:
            s = lax.dot_general(ks[pl.ds(0, kn), lane], qs[pl.ds(q0, qn), lane],
                                (((1,), (1,)), ((), ())), preferred_element_type=F32)
            later = lax.broadcasted_iota(jnp.int32, (qn, qn), 0) > lax.broadcasted_iota(
                jnp.int32, (qn, qn), 1)
            last = jnp.where(later, NEG, s[q0:])
            scores.append(jnp.concatenate([s[:q0], last], axis=0) if q0 else last)
        probs = []
        for s in scores:
            p = jnp.exp2((s - jnp.max(s, axis=0, keepdims=True)) * SCALE)
            probs.append((p.astype(BF), 1.0 / jnp.sum(p, axis=0, keepdims=True)))
        for (off, lane, q0, qn, kn), (p, inv) in zip(work, probs):
            o = inv * lax.dot_general(vs[pl.ds(0, kn), lane], p,
                                      (((0,), (0,)), ((), ())), preferred_element_type=F32)
            ctt[pl.ds(off, HD), pl.ds(q0, qn)] = o.astype(BF)
            ctx[pl.ds(q0, qn), lane] = o.T.astype(BF)
        return carry

    def heads(lo, hi):
        lax.fori_loop(lo // 4, hi // 4, attend, 0)

    def rows_of(zz, yy, cc):
        return pl.ds(pl.multiple_of((zz * 8 + yy * 2 + cc) * 160, 32), 160)

    every, both = pl.ds(0, 4), pl.ds(0, 2)
    halves = (pl.ds(0, D // 2), pl.ds(D // 2, D // 2))
    ah = (pl.ds(0, 2), pl.ds(2, 2))
    xp, xo, xm = ring(x, 1, 4), ring(x, 2, 4), ring(x, 3, 4)
    yp, yo, ym = ring(y, 1, 4), ring(y, 2, 4), ring(y, 3, 4)
    alld = pl.ds(0, D)
    sibs = []

    def zpos(s):
        zz = ring(z, s, 8)
        return zz // 4, lax.rem(zz, 4)

    c2 = [[], []]

    def zstep(step, strand):
        nxt = []
        for side in range(2):
            hh, ll = zpos(-step if side == 0 else step)
            if step:
                c2[strand][step - 1][side].wait_recv()
            if step < 4:
                part = ah[side] if step == 3 else every
                nxt.append(give(dz(1 if side == 0 else 7), hh, part, c, rc[strand], cols(ll)))
            if side == 0 or 0 < step < 4:
                if step < 4:
                    sibs.append(give(sib, hh, every, c, rc[strand], cols(ll)))
        if step == 4:
            hh, ll = zpos(4)
            sibs.append(give(sib, hh, every, c, rc[strand], cols(ll)))
        c2[strand].append(nxt)

    xs = []

    def context_across(blocks):
        for b in blocks:
            zz, yy = b // 4, b % 4
            xs.append(send(ctt.at[rows_of(zz, yy, oc)], cxo.at[zz, yy], sib))

    def grads(zz):
        for cp in xs[zz * 4:zz * 4 + 4]:
            cp.wait_recv()

        def tile(n, carry):
            lane = pl.ds(pl.multiple_of(n * 512, 128), 512)
            mine = jnp.concatenate([ctt[rows_of(zz, yy, c), :] for yy in range(4)], axis=0)
            acc = jnp.dot(mine, ct[:, lane], preferred_element_type=F32)
            acc += jnp.dot(cxo[zz].reshape(640, SEQ), cto[:, lane], preferred_element_type=F32)
            go[zz, :, :, lane] = acc.astype(BF).reshape(4, 160, 512)
            return carry

        lax.fori_loop(0, 5, tile, 0)

    def addf(*parts):
        total = parts[0].astype(F32)
        for part in parts[1:]:
            total = total + part.astype(F32)
        return total.astype(BF)

    s1, own, s2 = {}, {}, {}
    spans = [(pl.ds(lo, n), pl.ds(80 + lo, n)) for lo, n in CHUNKS]

    def first(k, zz):
        ga, gb = spans[k]
        fwd, back = (1, 3) if zz == 0 else (3, 1)
        bx, by = ring(x, back, 4), ring(y, back, 4)
        s1[k, zz] = (
            send(go.at[zz, every, ga, cols(xo)], r1x.at[zz, every, ga], dx(fwd)),
            send(go.at[zz, yo, gb, alld], r1y.at[zz, ga], dy(fwd)))
        own[k, zz] = (
            send(go.at[zz, every, ga, cols(bx)], r2x.at[1 - zz, zz, every, ga], dx(back)),
            send(go.at[zz, by, gb, alld], r2y.at[1 - zz, zz, ga], dy(back)))

    def second(k, zz):
        ga, gb = spans[k]
        fwd = 1 if zz == 0 else 3
        fx, fy = ring(x, fwd, 4), ring(y, fwd, 4)
        s1[k, zz][0].wait_recv()
        for yy in range(4):
            go[zz, yy, ga, cols(fx)] = addf(go[zz, yy, ga, cols(fx)], r1x[zz, yy, ga])
        a = send(go.at[zz, every, ga, cols(fx)], r2x.at[zz, zz, every, ga], dx(fwd))
        s1[k, zz][1].wait_recv()
        go[zz, fy, gb, :] = addf(go[zz, fy, gb, :], r1y[zz, ga])
        b = send(go.at[zz, fy, gb, alld], r2y.at[zz, zz, ga], dy(fwd))
        s2[k, zz] = (a, b)

    p2 = {}

    def third(k):
        ga, gb = spans[k]
        for zz in range(2):
            own[k, zz][0].wait_recv()
            s2[k, zz][0].wait_recv()
            for yy in range(4):
                go[zz, yy, ga, cols(x)] = addf(go[zz, yy, ga, cols(x)], r2x[0, zz, yy, ga], r2x[1, zz, yy, ga])
        pa = [send(go.at[both, ring(y, s, 4), ga, cols(x)], r3a.at[s - 1, both, ga], dy(s)) for s in (1, 3, 2)]
        for zz in range(2):
            own[k, zz][1].wait_recv()
            s2[k, zz][1].wait_recv()
            go[zz, y, gb, :] = addf(go[zz, y, gb, :], r2y[0, zz, ga], r2y[1, zz, ga])
        pb = [send(go.at[both, y, gb, cols(ring(x, s, 4))], r3b.at[s - 1, both, ga], dx(s)) for s in (1, 3, 2)]
        p2[k] = (pa, pb)

    def fourth(k):
        ga, gb = spans[k]
        for cp in p2[k][0]:
            cp.wait_recv()
        for zz in range(2):
            pc[zz, ga, :] = addf(go[zz, y, ga, cols(x)], *[r3a[s, zz, ga] for s in range(3)])
        for cp in p2[k][1]:
            cp.wait_recv()
        for zz in range(2):
            pc[zz, gb, :] = addf(go[zz, y, gb, cols(x)], *[r3b[s, zz, ga] for s in range(3)])

    par = lax.rem(z, 2)
    zbase = NSEM - 8

    def window(ll):
        return pl.ds(pl.multiple_of(ll * 40 - 8 * lax.rem(ll, 2), 16), 48)

    def along_z(i, odd):
        zz = lax.rem(z // 2 + i, 4) * 2 + odd
        hh, ll = zz // 4, lax.rem(zz, 4)
        slot = 2 * i + par
        return pltpu.make_async_remote_copy(
            src_ref=pc.at[hh, window(ll), :], dst_ref=rz.at[slot],
            send_sem=ss.at[zbase + 2 * i + odd], recv_sem=rs.at[zbase + slot],
            device_id=at(x, y, zz, c), device_id_type=MESH)

    def wave(odd):
        for i in (2, 1, 3):
            along_z(i, odd).start()

        @pl.when(par != odd)
        def _():
            along_z(0, odd).start()

    heads(0, 8)
    context_across([0, 1, 2])
    heads(8, 12)
    context_across([3])
    for cp in a2o:
        cp.wait_recv()
    a3o = [give(dx(1), zh, every, c, ra, cols(x)), give(dx(3), zh, every, c, ra, cols(x))]
    a1.wait_recv()
    a2t = [give(dy(s), oz, y, c, ra, cols(x)) for s in (1, 3, 2)]
    b2 = [give(dx(s), oz, y, c, rb, cols(x)) for s in (1, 3, 2)]
    tsend.wait_recv()
    grads(0)
    first(0, 0)
    for strand in range(2):
        for cp in c1[strand]:
            cp.wait_recv()
        zstep(0, strand)
    heads(12, 20)
    context_across([4, 5, 6, 7])
    for cp in b2:
        cp.wait_recv()
    b3t = [give(dy(1), oz, y, c, rb, alld), give(dy(3), oz, y, c, rb, alld)]
    b3o[0].wait_recv()
    fo = [give(dy(1), zh, ym, c, rb, halves[0])]
    b3o[1].wait_recv()
    fo.append(give(dy(3), zh, yp, c, rb, halves[1]))
    grads(1)
    first(0, 1)
    for cp in a2t:
        cp.wait_recv()
    a3t = [give(dx(1), oz, every, c, ra, cols(x)), give(dx(3), oz, every, c, ra, cols(x))]
    zstep(1, 0)
    a3o[0].wait_recv()
    fa = [give(dx(1), zh, ah[0], c, ra, cols(xm))]
    a3o[1].wait_recv()
    fa.append(give(dx(3), zh, ah[1], c, ra, cols(xp)))
    first(1, 0)
    second(0, 0)
    zstep(1, 1)
    second(0, 1)
    first(1, 1)
    for cp in b3t:
        cp.wait_recv()
    ft = [give(dy(1), oz, ym, c, rb, halves[0]), give(dy(3), oz, yp, c, rb, halves[1])]
    for cp in fo:
        cp.wait_recv()
    sibs.append(give(sib, zh, every, c, rb, alld))
    a3t[0].wait_recv()
    fa.append(give(dx(1), oz, ah[0], c, ra, cols(xm)))
    a3t[1].wait_recv()
    fa.append(give(dx(3), oz, ah[1], c, ra, cols(xp)))
    zstep(2, 0)
    second(1, 0)
    zstep(2, 1)
    second(1, 1)
    third(0)
    zstep(3, 0)
    for cp in ft:
        cp.wait_recv()
    sibs.append(give(sib, oz, every, c, rb, alld))
    for cp in fa:
        cp.wait_recv()
    sibs.append(give(sib, zh, every, c, ra, alld))
    sibs.append(give(sib, oz, every, c, ra, alld))
    zstep(3, 1)
    third(1)
    fourth(0)
    wave(0)
    zstep(4, 0)
    fourth(1)
    wave(1)
    zstep(4, 1)

    for cp in sibs:
        cp.wait_recv()
    for n in range(10):
        lane = pl.ds(n * 256, 256)
        w = wf[:, :, :, :, lane].reshape(D, 256)
        out_ref[:, lane] = jnp.dot(ctx[...], w, preferred_element_type=F32).astype(BF)

    for i in (1, 3, 2):
        for sender in range(2):
            pltpu.make_async_remote_copy(
                src_ref=rz.at[0], dst_ref=rz.at[2 * i + sender], send_sem=ss.at[zbase],
                recv_sem=rs.at[zbase + 2 * i + sender], device_id=dz(1), device_id_type=MESH).wait_recv()
    pltpu.make_async_remote_copy(
        src_ref=rz.at[0], dst_ref=rz.at[1 - par], send_sem=ss.at[zbase],
        recv_sem=rs.at[zbase + 1 - par], device_id=dz(1), device_id_type=MESH).wait_recv()
    total = pc[zh, window(zl), :].astype(F32) + rz[1 - par].astype(F32)
    for slot in range(2, 8):
        total = total + rz[slot].astype(F32)
    s3[...] = total

    mine = s3[pl.ds(pl.multiple_of(8 * lax.rem(zl, 2), 8), 40), :]
    snd[...] = jnp.zeros(snd.shape, F32)
    for t in range(4):
        snd[t, pl.ds(0, 10), :] = mine[10 * t:10 * t + 10, :]
    p4 = [send(snd.at[ring(x, s, 4)], r4.at[s - 1], dx(s)) for s in (1, 3, 2)]
    lm1.wait()
    lm2.wait()

    def adam(quarter, g):
        lane = cols(quarter)
        first_ref[:, lane] = 0.9 * m1[:, lane] + 0.1 * g
        second_ref[:, lane] = 0.95 * m2[:, lane] + 0.05 * g * g

    adam(x, snd[x, pl.ds(0, 10), :])
    for s, cp in zip((1, 3, 2), p4):
        cp.wait_recv()
        adam(ring(x, -s, 4), r4[s - 1, pl.ds(0, 10), :])
    for cp in sent:
        cp.wait_send()
    for odd in range(2):
        for i in (1, 2, 3):
            along_z(i, odd).wait_send()
    along_z(0, 1 - par).wait_send()
    assert count[0] <= zbase, count[0]


def on_device(*args):
    any_spec = pl.BlockSpec(memory_space=pl.ANY)
    V = pltpu.VMEM
    return pl.pallas_call(
        kernel,
        name="fused_layer",
        out_shape=(V((SEQ, D), BF), V((10, D), F32), V((10, D), F32)),
        in_specs=[any_spec] * 7,
        out_specs=(pl.BlockSpec(memory_space=V),) * 3,
        scratch_shapes=[
            V((SEQ, D), BF), V((SEQ, D), BF), V((SEQ, D), BF), V((SEQ, D), BF), V((SEQ, D), BF),
            V((SEQ, D), BF),
            V((D, SEQ), BF),
            V((2, 4, 160, SEQ), BF),
            V((2, 4, 2, 160, D), BF),
            V((2, 4, 160, D), BF),
            V((2, 4, 80, Q4), BF),
            V((2, 2, 4, 80, Q4), BF),
            V((2, 80, D), BF),
            V((2, 2, 80, D), BF),
            V((3, 2, 80, Q4), BF),
            V((3, 2, 80, Q4), BF),
            V((2, 160, Q4), BF),
            V((8, 48, Q4), BF),
            V((48, Q4), F32),
            V((4, 16, Q4), F32),
            V((3, 16, Q4), F32),
            V((10, D), F32), V((10, D), F32),
            pltpu.SemaphoreType.DMA((NSEM,)),
            pltpu.SemaphoreType.DMA((NSEM,)),
            pltpu.SemaphoreType.DMA((10,)),
        ],
        compiler_params=pltpu.CompilerParams(
            collective_id=0, has_side_effects=True, vmem_limit_bytes=60 * 2**20),
        cost_estimate=pl.CostEstimate(flops=15_000_000_000, bytes_accessed=14_000_000, transcendentals=2_600_000),
    )(*args)


def solution(mesh):
    rows = P(("blk", "rep"), None)
    return jax.shard_map(
        on_device, mesh=mesh, in_specs=(rows, rows, rows, rows, P("blk", None), rows, rows),
        out_specs=(rows, rows, rows), check_vma=False)
```

time: 119 us -> 90.1 us (0.76)
  Pallas kernels: 114 us -> 86.7 us
  local copies, waits for them, and re-layouts: 4.56 us -> 2.72 us
    pallas_call x1, Pallas kernels: 114 us -> 86.7 us  [on_device(): pl.pallas_call(kernel, name='fused_layer', out_shape=(V((SEQ, D), BF), V(...]
    unnamed x7 -> x3, local copies, waits for them, and re-layouts: 4.56 us -> 2.72 us
where the time goes in v2:
time: 90.1 us
  Pallas kernels  86.7 us (96%)
  local copies, waits for them, and re-layouts  2.72 us (3%)
    pallas_call x1, Pallas kernels, on_device(): pl.pallas_call(kernel, name='fused_layer', out_shape=(V((SEQ, D), BF), V(...  86.7 us
    unnamed x3, local copies, waits for them, and re-layouts  2.72 us

profile of v2, /device:TPU:1, one launch (start us, length us, event | category | flops | bytes accessed | tf_op | source)
XLA Modules:
  0.0 90.1 jit_solution(16195811337298780090)
XLA Ops:
  0.6 86.7 %fused_layer.1 = (bf16[448,2560]{1,0:T(8,128)(2,1)S(1)}, f32[10,2560]{1,0:T(8,128)S(1)}, f32[10,2560]{1,0:T(8,128)S(1)}) custom-call(bf16[448,2560]{1,0:T(8,128)(2,1)} %q_hbm.1, bf16[448,2560]{1,0:T(8,128)(2,1)} %k_hbm.1, bf16[448,2560]{1,0:T(8,128)(2,1)} %v_hbm.1, bf16[448,2560]{1,0:T(8,128)(2,1)} %t_hbm.1, bf16[160,2560]{1,0:T(8,128)(2,1)} %w_hbm.1, ...), custom_call_target="tpu_custom_call" | custom-call | flops 15000000512 | bytes 14000000 | tf_op jit(solution)/shard_map/fused_layer/pallas_call | solution.py:399
  87.3 1.4 %copy.13 = bf16[448,2560]{1,0:T(8,128)(2,1)} copy(bf16[448,2560]{1,0:T(8,128)(2,1)S(1)} %get-tuple-element.3) | data formatting | bytes 4587520
  88.7 0.7 copy.14
  89.4 0.7 copy.15

commit v3 on v2

--- a/solution.py
+++ b/solution.py
@@ -287,6 +287,7 @@
     tsend.wait_recv()
     grads(0)
     first(0, 0)
+    first(1, 0)
     for strand in range(2):
         for cp in c1[strand]:
             cp.wait_recv()
@@ -310,7 +311,6 @@
     fa = [give(dx(1), zh, ah[0], c, ra, cols(xm))]
     a3o[1].wait_recv()
     fa.append(give(dx(3), zh, ah[1], c, ra, cols(xp)))
-    first(1, 0)
     second(0, 0)
     zstep(1, 1)
     second(0, 1)
@@ -329,8 +329,8 @@
     second(1, 0)
     zstep(2, 1)
     second(1, 1)
+    zstep(3, 0)
     third(0)
-    zstep(3, 0)
     for cp in ft:
         cp.wait_recv()
     sibs.append(give(sib, oz, every, c, rb, alld))

time: 90.1 us -> 88.9 us (0.987); the launches traced: 90.1 us -> 87.2 us
  Pallas kernels: 86.7 us -> 83.8 us
    pallas_call x1, Pallas kernels: 86.7 us -> 83.8 us  [on_device(): pl.pallas_call(kernel, name='fused_layer', out_shape=(V((SEQ, D), BF), V(...]
where the time goes in v3:
time: 88.9 us; the launch traced here: 87.2 us
  Pallas kernels  83.8 us (94%)
  local copies, waits for them, and re-layouts  2.72 us (3%)
    pallas_call x1, Pallas kernels, on_device(): pl.pallas_call(kernel, name='fused_layer', out_shape=(V((SEQ, D), BF), V(...  83.8 us
    unnamed x3, local copies, waits for them, and re-layouts  2.72 us

profile of v3, /device:TPU:1, one launch (start us, length us, event | category | flops | bytes accessed | tf_op | source)
XLA Modules:
  0.0 87.2 jit_solution(13265471549557990904)
XLA Ops:
  0.6 83.8 %fused_layer.1 = (bf16[448,2560]{1,0:T(8,128)(2,1)S(1)}, f32[10,2560]{1,0:T(8,128)S(1)}, f32[10,2560]{1,0:T(8,128)S(1)}) custom-call(bf16[448,2560]{1,0:T(8,128)(2,1)} %q_hbm.1, bf16[448,2560]{1,0:T(8,128)(2,1)} %k_hbm.1, bf16[448,2560]{1,0:T(8,128)(2,1)} %v_hbm.1, bf16[448,2560]{1,0:T(8,128)(2,1)} %t_hbm.1, bf16[160,2560]{1,0:T(8,128)(2,1)} %w_hbm.1, ...), custom_call_target="tpu_custom_call" | custom-call | flops 15000000512 | bytes 14000000 | tf_op jit(solution)/shard_map/fused_layer/pallas_call | solution.py:399
  84.4 1.4 %copy.13 = bf16[448,2560]{1,0:T(8,128)(2,1)} copy(bf16[448,2560]{1,0:T(8,128)(2,1)S(1)} %get-tuple-element.3) | data formatting | bytes 4587520
  85.8 0.7 copy.14
  86.5 0.7 copy.15
